TPU v7x, 32 devices: a whole 2x2x4 slice. The times are simulated.
32 devices in a mesh: gx: 4 (over z), gy: 4 (over y, x), gz: 2 (over core).
Axes of the slice: x: 2, y: 2, z: 4, core: 2. Of those that a mesh axis runs over, the one named last changes fastest.
Arguments:
- tensor: float32 [512, 256, 256], P('gx', 'gy', 'gz'), may hold values from -60 to 60
- factor_a: float32 [512, 64], P(('gx', 'gy', 'gz')), may hold values from -6 to 6
- factor_b: float32 [256, 64], P(('gy', 'gx', 'gz')), may hold values from -6 to 6
- factor_c: float32 [256, 64], P(('gz', 'gx', 'gy')), may hold values from -6 to 6
Outputs:
- slope_a: float32 [512, 64], P(('gx', 'gy', 'gz'))
- slope_b: float32 [256, 64], P(('gy', 'gx', 'gz'))
- slope_c: float32 [256, 64], P(('gz', 'gx', 'gy'))
All inputs are finite; a program needn't handle non-finite values.
Results may differ from a plain program's by a relative error of at most 0.0003.
Values sent between devices are 32-bit elements; how exact they have to be, the bound alone decides.
A program may use at most 64 MiB of HBM per device.

v0:
```python
import jax
import jax.numpy as jnp
from jax import lax
from jax.sharding import PartitionSpec as P

STEPS = 2


step_size = 0.1


def gram_local(matrix):
    return jnp.dot(
        matrix.T, matrix, precision=lax.Precision.HIGHEST, preferred_element_type=jnp.float32
    )


def gather_blocks(own_a, own_b, own_c):
    block_a = lax.all_gather(own_a, ("gy", "gz"), axis=0, tiled=True)
    block_b = lax.all_gather(own_b, ("gx", "gz"), axis=0, tiled=True)
    block_c = lax.all_gather(own_c, ("gx", "gy"), axis=0, tiled=True)
    return (block_a, block_b, block_c)


def gram_sums(own_a, own_b, own_c):
    gram_a, gram_b, gram_c = lax.psum(
        (gram_local(own_a), gram_local(own_b), gram_local(own_c)), ("gx", "gy", "gz")
    )
    return (gram_a, gram_b, gram_c)


def partials(tensor, block_a, block_b, block_c):
    highest = lax.Precision.HIGHEST
    along_k = jnp.einsum("ijk,kr->jri", tensor, block_c, precision=highest)
    moment_a = jnp.einsum("jri,jr->ir", along_k, block_b, precision=highest)
    moment_b = jnp.einsum("jri,ir->jr", along_k, block_a, precision=highest)
    along_i = jnp.einsum("ijk,ir->rjk", tensor, block_a, precision=highest)
    moment_c = jnp.einsum("rjk,jr->kr", along_i, block_b, precision=highest)
    return (moment_a, moment_b, moment_c)


def slopes(first, second, third, moment_a, moment_b, moment_c, grams, counts):
    highest = lax.Precision.HIGHEST
    gram_a, gram_b, gram_c = grams
    count_i, count_j, count_k = counts
    slope_a = (jnp.dot(first, gram_b * gram_c, precision=highest) - moment_a) / (count_j * count_k)
    slope_b = (jnp.dot(second, gram_a * gram_c, precision=highest) - moment_b) / (count_i * count_k)
    slope_c = (jnp.dot(third, gram_a * gram_b, precision=highest) - moment_c) / (count_i * count_j)
    return (slope_a, slope_b, slope_c)


def shards(tensor, factor_a, factor_b, factor_c):
    counts = (
        float(tensor.shape[0] * lax.axis_size("gx")),
        float(tensor.shape[1] * lax.axis_size("gy")),
        float(tensor.shape[2] * lax.axis_size("gz")),
    )
    own_a, own_b, own_c = (factor_a, factor_b, factor_c)
    for round_index in range(STEPS):
        block_a, block_b, block_c = gather_blocks(own_a, own_b, own_c)
        grams = gram_sums(own_a, own_b, own_c)
        moment_a, moment_b, moment_c = partials(tensor, block_a, block_b, block_c)
        moment_a = lax.psum_scatter(moment_a, ("gy", "gz"), scatter_dimension=0, tiled=True)
        moment_b = lax.psum_scatter(moment_b, ("gx", "gz"), scatter_dimension=0, tiled=True)
        moment_c = lax.psum_scatter(moment_c, ("gx", "gy"), scatter_dimension=0, tiled=True)
        slope_a, slope_b, slope_c = slopes(
            own_a, own_b, own_c, moment_a, moment_b, moment_c, grams, counts
        )
        if round_index + 1 < STEPS:
            own_a = own_a - step_size * slope_a
            own_b = own_b - step_size * slope_b
            own_c = own_c - step_size * slope_c
    return (slope_a, slope_b, slope_c)


def solution(mesh):
    placed = (
        P("gx", "gy", "gz"),
        P(("gx", "gy", "gz"), None),
        P(("gy", "gx", "gz"), None),
        P(("gz", "gx", "gy"), None),
    )
    return jax.shard_map(
        shards,
        mesh=mesh,
        in_specs=placed,
        out_specs=(
            P(("gx", "gy", "gz"), None),
            P(("gy", "gx", "gz"), None),
            P(("gz", "gx", "gy"), None),
        ),
        check_vma=False,
    )
```

profile of v0, /device:TPU:0, one launch (start us, length us, event | category | flops | bytes accessed | tf_op | source)
XLA Modules:
  0.0 428.8 jit_solution(9458409411438681251)
XLA Ops:
  7.2 15.8 %all_gather.19 = f32[64,64]{1,0:T(8,128)S(1)} all-gather(f32[8,64]{1,0:T(8,128)} %param.6), channel_id=1, replica_groups=mesh['gx'=4,'gy'=4,'gz'=2] {'gx','gz'}, dimensions={0}, use_global_device_ids=true | all-gather | bytes 18432 | tf_op jit(solution)/shard_map/all_gather | solution.py:20
  23.0 41.3 %all_gather.18 = f32[128,64]{1,0:T(8,128)S(1)} all-gather(f32[8,64]{1,0:T(8,128)} %param.7), channel_id=1, replica_groups=mesh['gx'=4,'gy'=4,'gz'=2] {'gx','gy'}, dimensions={0}, use_global_device_ids=true | all-gather | bytes 34816 | tf_op jit(solution)/shard_map/all_gather | solution.py:21
  64.3 10.3 %fusion.9 = (f32[64,128]{1,0:T(8,128)S(1)}, f32[64,128,64]{1,0,2:T(8,128)}) fusion(f32[64,64]{0,1:T(8,128)S(1)} %bitcast.92, f32[128,64,128]{2,1,0:T(8,128)} %param.4, f32[128,64]{1,0:T(8,128)S(1)} %all_gather.18), kind=kOutput, calls=%fused_computation.11 | convolution fusion | flops 806346752 | bytes 6373376 | tf_op jit(solution)/shard_map/ijk,kr->jri/dot_general | solution.py:34
  76.2 7.8 %all_gather.20 = f32[128,64]{1,0:T(8,128)S(1)} all-gather(f32[16,64]{1,0:T(8,128)S(1)} %copy-done), channel_id=1, replica_groups=mesh['gx'=4,'gy'=4,'gz'=2] {'gy','gz'}, dimensions={0}, use_global_device_ids=true | all-gather | bytes 36864 | tf_op jit(solution)/shard_map/all_gather | solution.py:19
  84.0 7.2 %fusion.2 = f32[64,64,128]{2,0,1:T(8,128)S(1)} fusion(f32[128,64,128]{2,1,0:T(8,128)} %param.4, f32[128,64]{1,0:T(8,128)S(1)} %all_gather.20), kind=kOutput, calls=%fused_computation.2 | convolution fusion | flops 805306368 | bytes 6324224 | tf_op jit(solution)/shard_map/ijk,ir->rjk/dot_general | solution.py:37
  91.3 2.2 multiply_reduce_fusion.3
  93.6 26.1 %all-reduce = f32[64,64]{1,0:T(8,128)S(1)} all-reduce(f32[64,64]{1,0:T(8,128)S(1)} %bitcast.98), channel_id=3, replica_groups=mesh['gx'=4,'gy'=4,'gz'=2] {'gx','gz'}, use_global_device_ids=true, to_apply=%region_4.0.clone | all-reduce | flops 4096 | bytes 32768
  120.9 38.0 %all-reduce.5 = (f32[64,64]{1,0:T(8,128)S(1)}, f32[64,64]{1,0:T(8,128)S(1)}, f32[64,64]{1,0:T(8,128)S(1)}) all-reduce(f32[64,64]{1,0:T(8,128)S(1)} %fusion.34, f32[64,64]{1,0:T(8,128)S(1)} %fusion.32, f32[64,64]{1,0:T(8,128)S(1)} %fusion.33), channel_id=1, replica_groups=mesh['gx'=4,'gy'=4,'gz'=2] {'gx','gy','gz'}, use_global_device_ids=true, to_apply=%region_3.0 | all-reduce | flops 12288 | bytes 98304 | tf_op jit(solution)/shard_map/psum | solution.py:26
  159.4 2.4 multiply_reduce_fusion.2
  162.5 14.6 %all_gather.21 = f32[64,64]{1,0:T(8,128)S(1)} all-gather(f32[8,64]{1,0:T(8,128)S(1)} %fusion.21), channel_id=1, replica_groups=mesh['gx'=4,'gy'=4,'gz'=2] {'gx','gz'}, dimensions={0}, use_global_device_ids=true | all-gather | bytes 18432 | tf_op jit(solution)/shard_map/all_gather | solution.py:20
  178.5 0.8 fusion.13
  179.3 10.0 %all_gather.23 = f32[128,64]{1,0:T(8,128)S(1)} all-gather(f32[16,64]{1,0:T(8,128)S(1)} %fusion.13), channel_id=1, replica_groups=mesh['gx'=4,'gy'=4,'gz'=2] {'gy','gz'}, dimensions={0}, use_global_device_ids=true | all-gather | bytes 36864 | tf_op jit(solution)/shard_map/all_gather | solution.py:19
  189.4 7.2 %fusion = f32[64,64,128]{2,0,1:T(8,128)S(1)} fusion(f32[128,64,128]{2,1,0:T(8,128)} %param.4, f32[128,64]{1,0:T(8,128)S(1)} %all_gather.23), kind=kOutput, calls=%fused_computation | convolution fusion | flops 805306368 | bytes 6324224 | tf_op jit(solution)/shard_map/ijk,ir->rjk/dot_general | solution.py:37
  196.6 2.4 multiply_reduce_fusion
  199.0 0.7 copy.48
  200.1 103.7 %all-reduce.9.cloned.1.call-done = (f32[128,64]{1,0:T(8,128)}, f32[128,64]{1,0:T(8,128)}) async-done(((f32[128,64]{1,0:T(8,128)}, f32[128,64]{1,0:T(8,128)}), (f32[128,64]{1,0:T(8,128)}, f32[128,64]{1,0:T(8,128)})) %all-reduce.9.cloned.1.call-update) | async-done | bytes 65552
  303.8 0.8 fusion.18
  304.6 39.3 %all_gather.22 = f32[128,64]{1,0:T(8,128)S(1)} all-gather(f32[8,64]{1,0:T(8,128)S(1)} %fusion.18), channel_id=1, replica_groups=mesh['gx'=4,'gy'=4,'gz'=2] {'gx','gy'}, dimensions={0}, use_global_device_ids=true | all-gather | bytes 34816 | tf_op jit(solution)/shard_map/all_gather | solution.py:21
  344.1 9.3 %fusion.8 = (f32[64,128]{1,0:T(8,128)S(1)}, f32[64,128,64]{1,0,2:T(8,128)S(1)}) fusion(f32[64,64]{0,1:T(8,128)S(1)} %bitcast.91, f32[128,64,128]{2,1,0:T(8,128)} %param.4, f32[128,64]{1,0:T(8,128)S(1)} %all_gather.22), kind=kOutput, calls=%fused_computation.9 | convolution fusion | flops 806346752 | bytes 6373376 | tf_op jit(solution)/shard_map/ijk,kr->jri/dot_general | solution.py:34
  354.8 25.9 %all-reduce.2 = f32[64,64]{1,0:T(8,128)S(1)} all-reduce(f32[64,64]{1,0:T(8,128)S(1)} %bitcast.99), channel_id=6, replica_groups=mesh['gx'=4,'gy'=4,'gz'=2] {'gx','gz'}, use_global_device_ids=true, to_apply=%region_10.0.clone | all-reduce | flops 4096 | bytes 32768
  380.7 37.9 %all-reduce.4 = (f32[64,64]{1,0:T(8,128)S(1)}, f32[64,64]{1,0:T(8,128)S(1)}, f32[64,64]{1,0:T(8,128)S(1)}) all-reduce(f32[64,64]{1,0:T(8,128)S(1)} %fusion.35, f32[64,64]{1,0:T(8,128)S(1)} %fusion.36, f32[64,64]{1,0:T(8,128)S(1)} %fusion.37), channel_id=1, replica_groups=mesh['gx'=4,'gy'=4,'gz'=2] {'gx','gy','gz'}, use_global_device_ids=true, to_apply=%region_5.0 | all-reduce | flops 12288 | bytes 98304 | tf_op jit(solution)/shard_map/psum | solution.py:26
  418.6 0.7 fusion.15
  419.4 1.4 fusion.14
  420.8 1.4 fusion.10
  (35 shorter events, 6.0 us)
Async XLA Ops:
  7.2 171.3 %reduce-scatter.3.cloned.1.call-start = ((), (), s32[]{:S(2)}) async-start(), calls=%async_computation.2 | async-start | bytes 73728 | tf_op jit(solution)/shard_map/reduce_scatter | solution.py:63
  64.3 11.1 %copy-start.1 = (f32[8,64]{1,0:T(8,128)S(1)}, f32[8,64]{1,0:T(8,128)}, u32[]{:S(2)}) copy-start(f32[8,64]{1,0:T(8,128)} %param.6) | copy-start | bytes 6148
  64.3 11.4 %copy-start.2 = (f32[8,64]{1,0:T(8,128)S(1)}, f32[8,64]{1,0:T(8,128)}, u32[]{:S(2)}) copy-start(f32[8,64]{1,0:T(8,128)} %param.7) | copy-start | bytes 6148
  64.3 11.6 %copy-start = (f32[16,64]{1,0:T(8,128)S(1)}, f32[16,64]{1,0:T(8,128)}, u32[]{:S(2)}) copy-start(f32[16,64]{1,0:T(8,128)} %param.5) | copy-start | bytes 12292
  75.4 228.4 %all-reduce.9.cloned.1.call-start = ((), (), s32[]{:S(2)}) async-start(), calls=%async_computation.4 | async-start | bytes 262144
  91.3 28.5 %copy-start.4 = (u32[32]{0:T(128)S(1)}, u32[32]{0:T(128)}, u32[]{:S(2)}) copy-start(u32[32]{0:T(128)} %constant.28) | copy-start | bytes 388
  91.3 85.9 %copy-start.3 = (u32[32]{0:T(128)S(1)}, u32[32]{0:T(128)}, u32[]{:S(2)}) copy-start(u32[32]{0:T(128)} %constant.32) | copy-start | bytes 388
  199.7 221.1 %reduce-scatter.5.cloned.1.call-start = ((), (), s32[]{:S(2)}) async-start(), calls=%async_computation.3 | async-start | bytes 73728 | tf_op jit(solution)/shard_map/reduce_scatter | solution.py:63
Sparse Core Ops, SparseCore 0:
  75.5 29.1 reduce-scatter.2
  199.9 103.8 all-reduce.8
  354.3 29.0 reduce-scatter.4
where the time goes:
time: 430 us; the launch traced here: 429 us
  blocking collectives  257 us (60%)
  waiting for transfers between devices  104 us (24%)
  matrix products  40.9 us (10%)
  between operations  15.2 us (4%)
  other arithmetic  7.66 us (2%)
  local copies, waits for them, and re-layouts  4.34 us (1%)
    unnamed x4, waiting for transfers between devices  104 us
    all_gather x2, blocking collectives, gather_blocks(): block_c = lax.all_gather(own_c, ('gx', 'gy'), axis=0, tiled=True)  80.6 us
    psum x2, blocking collectives, gram_sums(): lax.psum((gram_local(own_a), gram_local(own_b), gram_local(own_c)), ('gx'...  75.9 us
    unnamed x2, blocking collectives  52.1 us
    all_gather x2, blocking collectives, gather_blocks(): block_b = lax.all_gather(own_b, ('gx', 'gz'), axis=0, tiled=True)  30.4 us
    dot_general x2, matrix products, partials(): along_k = jnp.einsum('ijk,kr->jri', tensor, block_c, precision=highest)  19.6 us
    all_gather x2, blocking collectives, gather_blocks(): block_a = lax.all_gather(own_a, ('gy', 'gz'), axis=0, tiled=True)  17.8 us
    dot_general x2, matrix products, partials(): along_i = jnp.einsum('ijk,ir->rjk', tensor, block_a, precision=highest)  14.4 us
  transfers between devices with their start and end apart: 3, of which 1 were waited for; matrix products, arithmetic and copies ran while one was open for 4% of the time, Pallas kernels for 0%

commit v1 on v0

v1 whole, which is shorter than its diff:
```python
import functools

import jax
import jax.numpy as jnp
from jax import lax
from jax.experimental import pallas as pl
from jax.experimental.pallas import tpu as pltpu
from jax.sharding import PartitionSpec as P

STEPS = 2
step_size = 0.1
HIGHEST = lax.Precision.HIGHEST
MESH = pl.DeviceIdType.MESH
CHUNK = 8


def twice(x):
    return jnp.concatenate([x, x], axis=1)


def left_half(shape):
    return lax.broadcasted_iota(jnp.int32, shape, 1) < shape[1] // 2


def split(x):
    high = x.astype(jnp.bfloat16).astype(jnp.float32)
    return high, x - high


def kernel(
    sizes,
    counts,
    tensor_hbm,
    own_a_ref,
    own_b_ref,
    own_c_ref,
    out_a_ref,
    out_b_ref,
    out_c_ref,
    tensor_ref,
    pair_ref,
    gat_a,
    gat_b,
    gat_c,
    blk_a,
    blk_b,
    blk_c,
    sum_a,
    sum_b,
    sum_c,
    push_a,
    push_b,
    push_c,
    pull_a,
    pull_b,
    pull_c,
    gram_a,
    gram_b,
    gram_c,
    load_sem,
    send_sem,
    recv_sem,
):
    nx, ny, nz = sizes
    gx, gy, gz = (lax.axis_index(name) for name in ("gx", "gy", "gz"))
    rank = own_a_ref.shape[1]
    wide = 2 * rank
    n_i, n_j, n_k = tensor_ref.shape
    n_chunks = n_i // CHUNK

    pieces = load_sem.shape[0]
    piece = n_i // pieces
    loads = [
        pltpu.make_async_copy(
            tensor_hbm.at[pl.ds(p * piece, piece)],
            tensor_ref.at[pl.ds(p * piece, piece)],
            load_sem.at[p],
        )
        for p in range(pieces)
    ]
    for load in loads:
        load.start()

    xs = [lax.rem(gx + d, nx) for d in range(nx)]
    ys = [lax.rem(gy + d, ny) for d in range(ny)]
    zs = [lax.rem(gz + d, nz) for d in range(nz)]

    def at(dx, dy, dz):
        return {"gx": xs[dx], "gy": ys[dy], "gz": zs[dz]}

    greeted = [
        (dx, dy, dz)
        for dx in range(nx)
        for dy in range(ny)
        for dz in range(nz)
        if 0 in (dx, dy, dz) and (dx or dy or dz)
    ]
    barrier = pltpu.get_barrier_semaphore()
    for offset in greeted:
        pl.semaphore_signal(barrier, inc=1, device_id=at(*offset), device_id_type=MESH)

    peers_a = [
        (at(0, dy, dz), ys[dy] * nz + zs[dz]) for dy in range(ny) for dz in range(nz) if dy or dz
    ]
    peers_b = [
        (at(dx, 0, dz), xs[dx] * nz + zs[dz]) for dx in range(nx) for dz in range(nz) if dx or dz
    ]
    peers_c = [
        (at(dx, dy, 0), xs[dx] * ny + ys[dy]) for dx in range(nx) for dy in range(ny) if dx or dy
    ]
    groups = (
        (peers_a, gy * nz + gz, 0),
        (peers_b, gx * nz + gz, 1),
        (peers_c, gx * ny + gy, 2),
    )
    lines = (
        ([(at(d, 0, 0), xs[d]) for d in range(1, nx)], gx, 0),
        ([(at(0, d, 0), ys[d]) for d in range(1, ny)], gy, 1),
        ([(at(0, 0, d), zs[d]) for d in range(1, nz)], gz, 2),
    )

    def transfer(src, dst, slot, device):
        return pltpu.make_async_remote_copy(
            src_ref=src,
            dst_ref=dst,
            send_sem=send_sem.at[slot],
            recv_sem=recv_sem.at[slot],
            device_id=device,
            device_id_type=MESH,
        )

    def all_of(buffer, peers, slot):
        some = buffer.at[pl.ds(0, len(peers))]
        return transfer(some, some, slot, peers[0][0])

    finals = []

    def gather(buffers, round_index, values):
        for (peers, me, which), buffer, value in zip(groups, buffers, values):
            slot = 9 * round_index + which
            buffer[round_index, me] = value
            for device, _ in peers:
                mine = buffer.at[round_index, me]
                transfer(mine, mine, slot, device).start()
            finals.append((buffer.at[round_index], peers, slot))

    gathers = (gat_a, gat_b, gat_c)
    own = [twice(ref[...]) for ref in (own_a_ref, own_b_ref, own_c_ref)]
    pl.semaphore_wait(barrier, len(greeted))
    gather(gathers, 0, own)

    for p, load in enumerate(loads):
        load.wait()

        def prepare(c, carry):
            block = tensor_ref[pl.ds(c * CHUNK, CHUNK)].reshape(CHUNK * n_j, n_k)
            high, low = split(block)
            rows = pl.ds(pl.multiple_of(c * (CHUNK * n_j), CHUNK * n_j), CHUNK * n_j)
            pair_ref[rows, pl.ds(0, n_k)] = high.astype(jnp.bfloat16)
            pair_ref[rows, pl.ds(n_k, n_k)] = low.astype(jnp.bfloat16)
            return carry

        lax.fori_loop(p * piece // CHUNK, (p + 1) * piece // CHUNK, prepare, 0)

    for round_index in range(STEPS):
        for (peers, me, which), buffer, block in zip(groups, gathers, (blk_a, blk_b, blk_c)):
            all_of(buffer.at[round_index], peers, 9 * round_index + which).wait_recv()
            rows = buffer.shape[2]
            for p in range(len(peers) + 1):
                block[p * rows : (p + 1) * rows] = buffer[round_index, p]

        half = rank // 2
        grams = (gram_a, gram_b, gram_c)
        for (peers, me, which), block, gram in zip(lines, (blk_a, blk_b, blk_c), grams):
            slot = 9 * round_index + 3 + which
            matrix = block[...]
            full = jnp.dot(
                matrix.T[:rank], matrix, precision=HIGHEST, preferred_element_type=jnp.float32
            )
            packed = jnp.where(left_half((half, wide)), full[:half], full[half:])
            gram[round_index, me] = packed
            for device, _ in peers:
                mine = gram.at[round_index, me]
                transfer(mine, mine, slot, device).start()
            finals.append((gram.at[round_index], peers, slot))

        block_b = blk_b[...]
        high_c, low_c = split(blk_c[...])
        mixed_c = jnp.where(left_half((n_k, wide)), high_c, low_c).astype(jnp.bfloat16)
        weights = jnp.concatenate([mixed_c, mixed_c], axis=0)

        sum_b[...] = jnp.zeros_like(sum_b)
        sum_c[...] = jnp.zeros_like(sum_c)

        def contract(c, carry):
            rows = pl.ds(pl.multiple_of(c * (CHUNK * n_j), CHUNK * n_j), CHUNK * n_j)
            pair = pair_ref[rows, :]
            part_a = pl.ds(pl.multiple_of(c * CHUNK, CHUNK), CHUNK)
            rows_a = blk_a[part_a, :]
            along = jnp.dot(pair, weights, preferred_element_type=jnp.float32)
            along = along.reshape(CHUNK, n_j, wide)
            sum_a[part_a, :] = jnp.sum(along * block_b[None], axis=1)
            sum_b[...] += jnp.sum(along * rows_a[:, None, :], axis=0)
            paired = (rows_a[:, None, :] * block_b[None]).reshape(CHUNK * n_j, wide)
            high, low = split(paired)
            mixed = jnp.where(left_half(paired.shape), high, low).astype(jnp.bfloat16)
            sum_c[...] += lax.dot_general(
                mixed, pair, (((0,), (0,)), ((), ())), preferred_element_type=jnp.float32
            )
            return carry

        lax.fori_loop(0, n_chunks, contract, 0)

        moment_a = sum_a[...]
        moment_b = sum_b[...]
        flipped = sum_c[...]
        flipped = flipped[:, :n_k] + flipped[:, n_k:]
        flipped = flipped[:rank] + flipped[rank:]
        moments = (
            moment_a + pltpu.roll(moment_a, rank, 1),
            moment_b + pltpu.roll(moment_b, rank, 1),
            jnp.concatenate([flipped, flipped], axis=0).T,
        )
        pushes, pulls = (push_a, push_b, push_c), (pull_a, pull_b, pull_c)
        for (peers, me, which), moment, push, pull in zip(groups, moments, pushes, pulls):
            slot = 9 * round_index + 6 + which
            rows = push.shape[2]
            for p in range(len(peers) + 1):
                push[round_index, p] = moment[p * rows : (p + 1) * rows]
            for device, place in peers:
                transfer(
                    push.at[round_index, place], pull.at[round_index, me], slot, device
                ).start()
            pull[round_index, me] = push[round_index, me]
            finals.append((pull.at[round_index], peers, slot))

        totals = []
        for (peers, me, which), gram in zip(lines, grams):
            all_of(gram.at[round_index], peers, 9 * round_index + 3 + which).wait_recv()
            totals.append(sum(gram[round_index, p] for p in range(len(peers) + 1)))

        def unpack(packed):
            turned = pltpu.roll(packed, rank, 1)
            left = left_half(packed.shape)
            return jnp.concatenate(
                [jnp.where(left, packed, turned), jnp.where(left, turned, packed)], axis=0
            )

        products = (
            unpack(totals[1] * totals[2]),
            unpack(totals[0] * totals[2]),
            unpack(totals[0] * totals[1]),
        )
        heads = [
            jnp.dot(x[:, :rank], product, precision=HIGHEST, preferred_element_type=jnp.float32)
            for x, product in zip(own, products)
        ]
        slopes = []
        for (peers, me, which), pull, head, count in zip(groups, pulls, heads, counts):
            all_of(pull.at[round_index], peers, 9 * round_index + 6 + which).wait_recv()
            moment = sum(pull[round_index, p] for p in range(len(peers) + 1))
            slopes.append((head - moment) / count)
        if round_index + 1 < STEPS:
            own = [x - step_size * slope for x, slope in zip(own, slopes)]
            gather(gathers, round_index + 1, own)

    for ref, slope in zip((out_a_ref, out_b_ref, out_c_ref), slopes):
        ref[...] = slope[:, :rank]
    for buffer, peers, slot in finals:
        all_of(buffer, peers, slot).wait_send()


def shards(sizes, tensor, factor_a, factor_b, factor_c):
    nx, ny, nz = sizes
    n_i, n_j, n_k = tensor.shape
    rank = factor_a.shape[1]
    wide = 2 * rank
    all_i, all_j, all_k = float(n_i * nx), float(n_j * ny), float(n_k * nz)
    counts = (all_j * all_k, all_i * all_k, all_i * all_j)
    f32 = jnp.float32
    rows = [x.shape[0] for x in (factor_a, factor_b, factor_c)]
    sides = [ny * nz, nx * nz, nx * ny]
    slots = [pltpu.VMEM((STEPS, n, r, wide), f32) for n, r in zip(sides, rows)]
    blocks = [pltpu.VMEM((n, wide), f32) for n in (n_i, n_j, n_k)]
    return pl.pallas_call(
        functools.partial(kernel, sizes, counts),
        out_shape=[jax.ShapeDtypeStruct(x.shape, f32) for x in (factor_a, factor_b, factor_c)],
        in_specs=[pl.BlockSpec(memory_space=pl.ANY)] + [pl.BlockSpec(memory_space=pltpu.VMEM)] * 3,
        out_specs=[pl.BlockSpec(memory_space=pltpu.VMEM)] * 3,
        scratch_shapes=[
            pltpu.VMEM(tensor.shape, f32),
            pltpu.VMEM((n_i * n_j, 2 * n_k), jnp.bfloat16),
            *slots,
            *blocks,
            pltpu.VMEM((n_i, wide), f32),
            pltpu.VMEM((n_j, wide), f32),
            pltpu.VMEM((wide, 2 * n_k), f32),
            *slots,
            *slots,
            *[pltpu.VMEM((STEPS, n, rank // 2, wide), f32) for n in sizes],
            pltpu.SemaphoreType.DMA((4,)),
            pltpu.SemaphoreType.DMA((9 * STEPS,)),
            pltpu.SemaphoreType.DMA((9 * STEPS,)),
        ],
        compiler_params=pltpu.CompilerParams(
            collective_id=0, has_side_effects=True, vmem_limit_bytes=48 * 1024 * 1024
        ),
    )(tensor, factor_a, factor_b, factor_c)


def solution(mesh):
    sizes = tuple(mesh.shape[name] for name in ("gx", "gy", "gz"))
    rows = (
        P(("gx", "gy", "gz"), None),
        P(("gy", "gx", "gz"), None),
        P(("gz", "gx", "gy"), None),
    )
    return jax.shard_map(
        functools.partial(shards, sizes),
        mesh=mesh,
        in_specs=(P("gx", "gy", "gz"), *rows),
        out_specs=rows,
        check_vma=False,
    )
```

time: 430 us -> 45.1 us (0.10)
  blocking collectives: 257 us -> 0 us
  waiting for transfers between devices: 104 us -> 0 us
  matrix products: 40.9 us -> 0 us
  Pallas kernels: 0 us -> 38.2 us
  between operations: 15.2 us -> 0.65 us
  other arithmetic: 7.66 us -> 0 us
    all_gather x6 -> x0, blocking collectives: 129 us -> none  [the longest x2 80.6 us: gather_blocks(): block_c = lax.all_gather(own_c, ('gx', 'gy'), axis=0, tiled=True)]
    unnamed x4 -> x0, waiting for transfers between devices: 104 us -> none
    psum x2 -> x0, blocking collectives: 75.9 us -> none  [gram_sums(): lax.psum((gram_local(own_a), gram_local(own_b), gram_local(own_c)), ('gx'...]
    unnamed x2 -> x0, blocking collectives: 52.1 us -> none
    dot_general x16 -> x0, matrix products: 40.9 us -> none  [the longest x2 19.6 us: partials(): along_k = jnp.einsum('ijk,kr->jri', tensor, block_c, precision=highest)]
    pallas_call x0 -> x1, Pallas kernels: none -> 38.2 us  [shards(): pl.pallas_call(functools.partial(kernel, sizes, counts), out_shape=[jax.S...]
    unnamed x2 -> x0, other arithmetic: 4.83 us -> none
    unnamed x16 -> x11, local copies, waits for them, and re-layouts: 1.47 us -> 6.04 us
  transfers between devices with their start and end apart: 3 -> 0, of which waited for: 1 -> 0; matrix products, arithmetic and copies ran while one was open for 4% -> 0% of each run, Pallas kernels for 0% -> 0%
where the time goes in v1:
time: 45.1 us; the launch traced here: 44.9 us
  Pallas kernels  38.2 us (85%)
  local copies, waits for them, and re-layouts  6.04 us (13%)
  between operations  0.65 us (1%)
    pallas_call x1, Pallas kernels, shards(): pl.pallas_call(functools.partial(kernel, sizes, counts), out_shape=[jax.S...  38.2 us
    unnamed x11, local copies, waits for them, and re-layouts  6.04 us

profile of v1, /device:TPU:0, one launch (start us, length us, event | category | flops | bytes accessed | tf_op | source)
XLA Modules:
  0.0 44.9 jit_solution(4775848398779025203)
XLA Ops:
  0.6 0.0 copy-start
  0.6 2.2 %copy-done = f32[128,64,128]{2,1,0:T(8,128)S(1)} copy-done((f32[128,64,128]{2,1,0:T(8,128)S(1)}, f32[128,64,128]{2,1,0:T(8,128)}, u32[]{:S(2)}) %copy-start) | copy-done | bytes 4194328
  2.8 0.0 copy-start.1
  2.8 0.7 %copy-done.1 = f32[16,64]{1,0:T(8,128)S(1)} copy-done((f32[16,64]{1,0:T(8,128)S(1)}, f32[16,64]{1,0:T(8,128)}, u32[]{:S(2)}) %copy-start.1) | copy-done | bytes 4120
  3.5 0.0 copy-start.2
  3.5 0.7 %copy-done.2 = f32[8,64]{1,0:T(8,128)S(1)} copy-done((f32[8,64]{1,0:T(8,128)S(1)}, f32[8,64]{1,0:T(8,128)}, u32[]{:S(2)}) %copy-start.2) | copy-done | bytes 2072
  4.2 0.0 copy-start.3
  4.2 0.7 %copy-done.3 = f32[8,64]{1,0:T(8,128)S(1)} copy-done((f32[8,64]{1,0:T(8,128)S(1)}, f32[8,64]{1,0:T(8,128)}, u32[]{:S(2)}) %copy-start.3) | copy-done | bytes 2072
  4.9 38.2 %shard_map.67 = (f32[16,64]{1,0:T(8,128)S(1)}, f32[8,64]{1,0:T(8,128)S(1)}, f32[8,64]{1,0:T(8,128)S(1)}) custom-call(f32[128,64,128]{2,1,0:T(8,128)S(1)} %copy-done, f32[16,64]{1,0:T(8,128)S(1)} %copy-done.1, f32[8,64]{1,0:T(8,128)S(1)} %copy-done.2, f32[8,64]{1,0:T(8,128)S(1)} %copy-done.3), custom_call_target="tpu_custom_call" | custom-call | tf_op jit(solution)/shard_map/pallas_call | solution.py:285
  43.1 0.6 %copy.10 = f32[16,64]{1,0:T(8,128)} copy(f32[16,64]{1,0:T(8,128)S(1)} %get-tuple-element.6) | data formatting | bytes 8192
  43.7 0.6 %copy.11 = f32[8,64]{1,0:T(8,128)} copy(f32[8,64]{1,0:T(8,128)S(1)} %get-tuple-element.7) | data formatting | bytes 4096
  44.3 0.6 %copy.12 = f32[8,64]{1,0:T(8,128)} copy(f32[8,64]{1,0:T(8,128)S(1)} %get-tuple-element.8) | data formatting | bytes 4096
Async XLA Ops:
  0.6 2.2 %copy-start = (f32[128,64,128]{2,1,0:T(8,128)S(1)}, f32[128,64,128]{2,1,0:T(8,128)}, u32[]{:S(2)}) copy-start(f32[128,64,128]{2,1,0:T(8,128)} %tensor_hbm.1) | copy-start | bytes 12582916
  2.8 0.7 %copy-start.1 = (f32[16,64]{1,0:T(8,128)S(1)}, f32[16,64]{1,0:T(8,128)}, u32[]{:S(2)}) copy-start(f32[16,64]{1,0:T(8,128)} %own_a_ref.1) | copy-start | bytes 12292
  3.5 0.7 %copy-start.2 = (f32[8,64]{1,0:T(8,128)S(1)}, f32[8,64]{1,0:T(8,128)}, u32[]{:S(2)}) copy-start(f32[8,64]{1,0:T(8,128)} %own_b_ref.1) | copy-start | bytes 6148
  4.2 0.7 %copy-start.3 = (f32[8,64]{1,0:T(8,128)S(1)}, f32[8,64]{1,0:T(8,128)}, u32[]{:S(2)}) copy-start(f32[8,64]{1,0:T(8,128)} %own_c_ref.1) | copy-start | bytes 6148

commit v2 on v1

v2 whole, which is shorter than its diff:
```python
import functools

import jax
import jax.numpy as jnp
from jax import lax
from jax.experimental import pallas as pl
from jax.experimental.pallas import tpu as pltpu
from jax.sharding import PartitionSpec as P

STEPS = 2
step_size = 0.1
HIGHEST = lax.Precision.HIGHEST
MESH = pl.DeviceIdType.MESH
CHUNK = 8
CHUNK_C = 16


def twice(x):
    return jnp.concatenate([x, x], axis=1)


def left_half(shape):
    return lax.broadcasted_iota(jnp.int32, shape, 1) < shape[1] // 2


def packed_rows(rows):
    return rows // 2 if rows % 2 == 0 else rows


def pack(x):
    rows = x.shape[0]
    if rows % 2:
        return x
    return jnp.where(left_half((rows // 2, x.shape[1])), x[: rows // 2], x[rows // 2 :])


def unpack(x, rows):
    if rows % 2:
        return (x,)
    turned = pltpu.roll(x, x.shape[1] // 2, 1)
    left = left_half(x.shape)
    return (jnp.where(left, x, turned), jnp.where(left, turned, x))


def split(x):
    high = x.astype(jnp.bfloat16).astype(jnp.float32)
    return high, x - high


def kernel(
    sizes,
    counts,
    tensor_hbm,
    own_a_hbm,
    own_b_hbm,
    own_c_hbm,
    out_a_ref,
    out_b_ref,
    out_c_ref,
    own_a_ref,
    own_b_ref,
    own_c_ref,
    tensor_ref,
    pair_ref,
    gat_a,
    gat_b,
    gat_c,
    blk_a,
    blk_b,
    blk_c,
    sum_a,
    sum_b,
    sum_c,
    push_a,
    push_b,
    push_c,
    pull_a,
    pull_b,
    pull_c,
    gram_a,
    gram_b,
    gram_c,
    own_sem,
    load_sem,
    send_sem,
    recv_sem,
):
    nx, ny, nz = sizes
    gx, gy, gz = (lax.axis_index(name) for name in ("gx", "gy", "gz"))
    rank = own_a_ref.shape[1]
    wide = 2 * rank
    n_i, n_j, n_k = tensor_ref.shape

    owned = (own_a_ref, own_b_ref, own_c_ref)
    own_loads = [
        pltpu.make_async_copy(hbm, ref, own_sem.at[p])
        for p, (hbm, ref) in enumerate(zip((own_a_hbm, own_b_hbm, own_c_hbm), owned))
    ]
    for load in own_loads:
        load.start()

    pieces = load_sem.shape[0]
    piece = n_i // pieces
    loads = [
        pltpu.make_async_copy(
            tensor_hbm.at[pl.ds(p * piece, piece)],
            tensor_ref.at[pl.ds(p * piece, piece)],
            load_sem.at[p],
        )
        for p in range(pieces)
    ]
    for load in loads:
        load.start()

    xs = [lax.rem(gx + d, nx) for d in range(nx)]
    ys = [lax.rem(gy + d, ny) for d in range(ny)]
    zs = [lax.rem(gz + d, nz) for d in range(nz)]

    def at(dx, dy, dz):
        return {"gx": xs[dx], "gy": ys[dy], "gz": zs[dz]}

    greeted = [
        (dx, dy, dz)
        for dx in range(nx)
        for dy in range(ny)
        for dz in range(nz)
        if 0 in (dx, dy, dz) and (dx or dy or dz)
    ]
    barrier = pltpu.get_barrier_semaphore()
    for offset in greeted:
        pl.semaphore_signal(barrier, inc=1, device_id=at(*offset), device_id_type=MESH)

    peers_a = [
        (at(0, dy, dz), ys[dy] * nz + zs[dz]) for dy in range(ny) for dz in range(nz) if dy or dz
    ]
    peers_b = [
        (at(dx, 0, dz), xs[dx] * nz + zs[dz]) for dx in range(nx) for dz in range(nz) if dx or dz
    ]
    peers_c = [
        (at(dx, dy, 0), xs[dx] * ny + ys[dy]) for dx in range(nx) for dy in range(ny) if dx or dy
    ]
    groups = (
        (peers_a, gy * nz + gz, 0),
        (peers_b, gx * nz + gz, 1),
        (peers_c, gx * ny + gy, 2),
    )
    lines = (
        ([(at(d, 0, 0), xs[d]) for d in range(1, nx)], gx, 0),
        ([(at(0, d, 0), ys[d]) for d in range(1, ny)], gy, 1),
        ([(at(0, 0, d), zs[d]) for d in range(1, nz)], gz, 2),
    )

    def transfer(src, dst, slot, device):
        return pltpu.make_async_remote_copy(
            src_ref=src,
            dst_ref=dst,
            send_sem=send_sem.at[slot],
            recv_sem=recv_sem.at[slot],
            device_id=device,
            device_id_type=MESH,
        )

    def all_of(buffer, peers, slot):
        some = buffer.at[pl.ds(0, len(peers))]
        return transfer(some, some, slot, peers[0][0])

    finals = []

    def gather(buffers, round_index, values):
        for (peers, me, which), buffer, value in zip(groups, buffers, values):
            slot = 9 * round_index + which
            buffer[round_index, me] = pack(value)
            for device, _ in peers:
                mine = buffer.at[round_index, me]
                transfer(mine, mine, slot, device).start()
            finals.append((buffer.at[round_index], peers, slot))

    gathers = (gat_a, gat_b, gat_c)
    for load in own_loads:
        load.wait()
    own = [twice(ref[...]) for ref in owned]
    pl.semaphore_wait(barrier, len(greeted))
    gather(gathers, 0, own)

    for p, load in enumerate(loads):
        load.wait()

        def prepare(c, carry):
            block = tensor_ref[pl.ds(c * CHUNK, CHUNK)].reshape(CHUNK * n_j, n_k)
            high, low = split(block)
            rows = pl.ds(pl.multiple_of(c * (CHUNK * n_j), CHUNK * n_j), CHUNK * n_j)
            pair_ref[rows, pl.ds(0, n_k)] = high.astype(jnp.bfloat16)
            pair_ref[rows, pl.ds(n_k, n_k)] = low.astype(jnp.bfloat16)
            return carry

        lax.fori_loop(p * piece // CHUNK, (p + 1) * piece // CHUNK, prepare, 0)

    blocks = (blk_a, blk_b, blk_c)
    grams = (gram_a, gram_b, gram_c)
    pushes, pulls = (push_a, push_b, push_c), (pull_a, pull_b, pull_c)
    half = rank // 2

    def receive(round_index, which):
        peers, me, _ = groups[which]
        buffer, block = gathers[which], blocks[which]
        all_of(buffer.at[round_index], peers, 9 * round_index + which).wait_recv()
        rows = owned[which].shape[0]
        for p in range(len(peers) + 1):
            parts = unpack(buffer[round_index, p], rows)
            step = rows // len(parts)
            for q, part in enumerate(parts):
                block[p * rows + q * step : p * rows + (q + 1) * step] = part

    def send_gram(round_index, which):
        peers, me, _ = lines[which]
        gram, slot = grams[which], 9 * round_index + 3 + which
        matrix = blocks[which][...]
        full = jnp.dot(
            matrix.T[:rank], matrix, precision=HIGHEST, preferred_element_type=jnp.float32
        )
        gram[round_index, me] = pack(full)
        for device, _ in peers:
            mine = gram.at[round_index, me]
            transfer(mine, mine, slot, device).start()
        finals.append((gram.at[round_index], peers, slot))

    def scatter(round_index, which, moment):
        peers, me, _ = groups[which]
        push, pull, slot = pushes[which], pulls[which], 9 * round_index + 6 + which
        rows = owned[which].shape[0]
        for p in range(len(peers) + 1):
            push[round_index, p] = pack(moment[p * rows : (p + 1) * rows])
        for device, place in peers:
            transfer(push.at[round_index, place], pull.at[round_index, me], slot, device).start()
        pull[round_index, me] = push[round_index, me]
        finals.append((pull.at[round_index], peers, slot))

    for round_index in range(STEPS):
        receive(round_index, 0)
        receive(round_index, 1)
        send_gram(round_index, 0)
        send_gram(round_index, 1)
        block_b = blk_b[...]

        sum_c[...] = jnp.zeros_like(sum_c)

        def contract_c(c, carry):
            rows = pl.ds(pl.multiple_of(c * (CHUNK_C * n_j), CHUNK_C * n_j), CHUNK_C * n_j)
            rows_a = blk_a[pl.ds(pl.multiple_of(c * CHUNK_C, CHUNK_C), CHUNK_C), :]
            paired = (rows_a[:, None, :] * block_b[None]).reshape(CHUNK_C * n_j, wide)
            high, low = split(paired)
            mixed = jnp.where(left_half(paired.shape), high, low).astype(jnp.bfloat16)
            sum_c[...] += lax.dot_general(
                mixed,
                pair_ref[rows, :],
                (((0,), (0,)), ((), ())),
                preferred_element_type=jnp.float32,
            )
            return carry

        lax.fori_loop(0, n_i // CHUNK_C, contract_c, 0, unroll=2)
        flipped = sum_c[...]
        flipped = flipped[:, :n_k] + flipped[:, n_k:]
        flipped = flipped[:rank] + flipped[rank:]
        scatter(round_index, 2, jnp.concatenate([flipped, flipped], axis=0).T)

        receive(round_index, 2)
        send_gram(round_index, 2)
        high_c, low_c = split(blk_c[...])
        mixed_c = jnp.where(left_half((n_k, wide)), high_c, low_c).astype(jnp.bfloat16)
        weights = jnp.concatenate([mixed_c, mixed_c], axis=0)
        sum_b[...] = jnp.zeros_like(sum_b)

        def contract_ab(c, carry):
            rows = pl.ds(pl.multiple_of(c * (CHUNK * n_j), CHUNK * n_j), CHUNK * n_j)
            part_a = pl.ds(pl.multiple_of(c * CHUNK, CHUNK), CHUNK)
            rows_a = blk_a[part_a, :]
            along = jnp.dot(pair_ref[rows, :], weights, preferred_element_type=jnp.float32)
            along = along.reshape(CHUNK, n_j, wide)
            sum_a[part_a, :] = jnp.sum(along * block_b[None], axis=1)
            sum_b[...] += jnp.sum(along * rows_a[:, None, :], axis=0)
            return carry

        lax.fori_loop(0, n_i // CHUNK, contract_ab, 0, unroll=4)
        moment_a, moment_b = sum_a[...], sum_b[...]
        scatter(round_index, 0, moment_a + pltpu.roll(moment_a, rank, 1))
        scatter(round_index, 1, moment_b + pltpu.roll(moment_b, rank, 1))

        totals = []
        for (peers, me, which), gram in zip(lines, grams):
            all_of(gram.at[round_index], peers, 9 * round_index + 3 + which).wait_recv()
            totals.append(sum(gram[round_index, p] for p in range(len(peers) + 1)))
        products = [
            jnp.concatenate(unpack(totals[p] * totals[q], rank), axis=0)
            for p, q in ((1, 2), (0, 2), (0, 1))
        ]
        heads = [
            jnp.dot(x[:, :rank], product, precision=HIGHEST, preferred_element_type=jnp.float32)
            for x, product in zip(own, products)
        ]
        slopes = [None] * 3
        for which in (2, 0, 1):
            peers = groups[which][0]
            pull, rows = pulls[which], owned[which].shape[0]
            all_of(pull.at[round_index], peers, 9 * round_index + 6 + which).wait_recv()
            moment = sum(pull[round_index, p] for p in range(len(peers) + 1))
            moment = jnp.concatenate(unpack(moment, rows), axis=0)
            slopes[which] = (heads[which] - moment) / counts[which]
        if round_index + 1 < STEPS:
            own = [x - step_size * slope for x, slope in zip(own, slopes)]
            gather(gathers, round_index + 1, own)

    for ref, slope in zip((out_a_ref, out_b_ref, out_c_ref), slopes):
        ref[...] = slope[:, :rank]
    for buffer, peers, slot in finals:
        all_of(buffer, peers, slot).wait_send()


def store(from_a, from_b, from_c, to_a, to_b, to_c, sem):
    copies = [
        pltpu.make_async_copy(source, target, sem.at[p])
        for p, (source, target) in enumerate(((from_a, to_a), (from_b, to_b), (from_c, to_c)))
    ]
    for copy in copies:
        copy.start()
    for copy in copies:
        copy.wait()


def shards(sizes, tensor, factor_a, factor_b, factor_c):
    nx, ny, nz = sizes
    n_i, n_j, n_k = tensor.shape
    rank = factor_a.shape[1]
    wide = 2 * rank
    all_i, all_j, all_k = float(n_i * nx), float(n_j * ny), float(n_k * nz)
    counts = (all_j * all_k, all_i * all_k, all_i * all_j)
    f32 = jnp.float32
    rows = [x.shape[0] for x in (factor_a, factor_b, factor_c)]
    sides = [ny * nz, nx * nz, nx * ny]
    slots = [pltpu.VMEM((STEPS, n, packed_rows(r), wide), f32) for n, r in zip(sides, rows)]
    blocks = [pltpu.VMEM((n, wide), f32) for n in (n_i, n_j, n_k)]
    slopes = pl.pallas_call(
        functools.partial(kernel, sizes, counts),
        out_shape=[jax.ShapeDtypeStruct(x.shape, f32) for x in (factor_a, factor_b, factor_c)],
        in_specs=[pl.BlockSpec(memory_space=pltpu.HBM)] * 4,
        out_specs=[pl.BlockSpec(memory_space=pltpu.VMEM)] * 3,
        scratch_shapes=[
            *[pltpu.VMEM(x.shape, f32) for x in (factor_a, factor_b, factor_c)],
            pltpu.VMEM(tensor.shape, f32),
            pltpu.VMEM((n_i * n_j, 2 * n_k), jnp.bfloat16),
            *slots,
            *blocks,
            pltpu.VMEM((n_i, wide), f32),
            pltpu.VMEM((n_j, wide), f32),
            pltpu.VMEM((wide, 2 * n_k), f32),
            *slots,
            *slots,
            *[pltpu.VMEM((STEPS, n, rank // 2, wide), f32) for n in sizes],
            pltpu.SemaphoreType.DMA((3,)),
            pltpu.SemaphoreType.DMA((4,)),
            pltpu.SemaphoreType.DMA((9 * STEPS,)),
            pltpu.SemaphoreType.DMA((9 * STEPS,)),
        ],
        compiler_params=pltpu.CompilerParams(
            collective_id=0, has_side_effects=True, vmem_limit_bytes=60 * 1024 * 1024
        ),
    )(tensor, factor_a, factor_b, factor_c)
    return pl.pallas_call(
        store,
        out_shape=[jax.ShapeDtypeStruct(x.shape, f32) for x in (factor_a, factor_b, factor_c)],
        in_specs=[pl.BlockSpec(memory_space=pl.ANY)] * 3,
        out_specs=[pl.BlockSpec(memory_space=pltpu.HBM)] * 3,
        scratch_shapes=[pltpu.SemaphoreType.DMA((3,))],
        compiler_params=pltpu.CompilerParams(vmem_limit_bytes=60 * 1024 * 1024),
    )(*slopes)


def solution(mesh):
    sizes = tuple(mesh.shape[name] for name in ("gx", "gy", "gz"))
    rows = (
        P(("gx", "gy", "gz"), None),
        P(("gy", "gx", "gz"), None),
        P(("gz", "gx", "gy"), None),
    )
    return jax.shard_map(
        functools.partial(shards, sizes),
        mesh=mesh,
        in_specs=(P("gx", "gy", "gz"), *rows),
        out_specs=rows,
        check_vma=False,
    )
```

time: 45.1 us -> 33.4 us (0.74)
  local copies, waits for them, and re-layouts: 6.04 us -> 0 us
  Pallas kernels: 38.2 us -> 32.6 us
    pallas_call x1, Pallas kernels: 38.2 us -> 31 us  [shards(): pl.pallas_call(functools.partial(kernel, sizes, counts), out_shape=[jax.S...]
    unnamed x11 -> x0, local copies, waits for them, and re-layouts: 6.04 us -> none
    pallas_call x0 -> x1, Pallas kernels: none -> 1.63 us  [shards(): pl.pallas_call(store, out_shape=[jax.ShapeDtypeStruct(x.shape, f32) for x...]
where the time goes in v2:
time: 33.4 us; the launch traced here: 33.3 us
  Pallas kernels  32.6 us (98%)
  between operations  0.64 us (2%)
    pallas_call x1, Pallas kernels, shards(): pl.pallas_call(functools.partial(kernel, sizes, counts), out_shape=[jax.S...  31 us
    pallas_call x1, Pallas kernels, shards(): pl.pallas_call(store, out_shape=[jax.ShapeDtypeStruct(x.shape, f32) for x...  1.63 us

profile of v2, /device:TPU:0, one launch (start us, length us, event | category | flops | bytes accessed | tf_op | source)
XLA Modules:
  0.0 33.3 jit_solution(8189151916890239864)
XLA Ops:
  0.6 31.0 %shard_map.67 = (f32[16,64]{1,0:T(8,128)}, f32[8,64]{1,0:T(8,128)}, f32[8,64]{1,0:T(8,128)}) custom-call(f32[128,64,128]{2,1,0:T(8,128)} %tensor_hbm.1, f32[16,64]{1,0:T(8,128)} %own_a_hbm.1, f32[8,64]{1,0:T(8,128)} %own_b_hbm.1, f32[8,64]{1,0:T(8,128)} %own_c_hbm.1), custom_call_target="tpu_custom_call" | custom-call | tf_op jit(solution)/shard_map/pallas_call | solution.py:342
  31.6 1.6 %shard_map.68 = (f32[16,64]{1,0:T(8,128)}, f32[8,64]{1,0:T(8,128)}, f32[8,64]{1,0:T(8,128)}) custom-call(f32[16,64]{1,0:T(8,128)} %get-tuple-element.6.from_a, f32[8,64]{1,0:T(8,128)} %get-tuple-element.7.from_b, f32[8,64]{1,0:T(8,128)} %get-tuple-element.8.from_c), custom_call_target="tpu_custom_call" | custom-call | tf_op jit(solution)/shard_map/pallas_call | solution.py:368

commit v3 on v2

--- a/solution.py
+++ b/solution.py
@@ -9,7 +9,6 @@
 
 STEPS = 2
 step_size = 0.1
-HIGHEST = lax.Precision.HIGHEST
 MESH = pl.DeviceIdType.MESH
 CHUNK = 8
 CHUNK_C = 16
@@ -45,6 +44,11 @@
 def split(x):
     high = x.astype(jnp.bfloat16).astype(jnp.float32)
     return high, x - high
+
+
+def mix(x):
+    high, low = split(x)
+    return jnp.where(left_half(x.shape), high, low).astype(jnp.bfloat16)
 
 
 def kernel(
@@ -166,21 +170,23 @@
 
     finals = []
 
-    def gather(buffers, round_index, values):
-        for (peers, me, which), buffer, value in zip(groups, buffers, values):
-            slot = 9 * round_index + which
-            buffer[round_index, me] = pack(value)
-            for device, _ in peers:
-                mine = buffer.at[round_index, me]
-                transfer(mine, mine, slot, device).start()
-            finals.append((buffer.at[round_index], peers, slot))
-
     gathers = (gat_a, gat_b, gat_c)
+
+    def gather(round_index, which, value):
+        peers, me, _ = groups[which]
+        buffer, slot = gathers[which], 9 * round_index + which
+        buffer[round_index, me] = pack(value)
+        for device, _ in peers:
+            mine = buffer.at[round_index, me]
+            transfer(mine, mine, slot, device).start()
+        finals.append((buffer.at[round_index], peers, slot))
+
     for load in own_loads:
         load.wait()
     own = [twice(ref[...]) for ref in owned]
     pl.semaphore_wait(barrier, len(greeted))
-    gather(gathers, 0, own)
+    for which in range(3):
+        gather(0, which, own[which])
 
     for p, load in enumerate(loads):
         load.wait()
@@ -214,10 +220,12 @@
     def send_gram(round_index, which):
         peers, me, _ = lines[which]
         gram, slot = grams[which], 9 * round_index + 3 + which
-        matrix = blocks[which][...]
-        full = jnp.dot(
-            matrix.T[:rank], matrix, precision=HIGHEST, preferred_element_type=jnp.float32
+        mixed = mix(blocks[which][...])
+        full = lax.dot_general(
+            mixed, mixed, (((0,), (0,)), ((), ())), preferred_element_type=jnp.float32
         )
+        full = full[:rank] + full[rank:]
+        full = full + pltpu.roll(full, rank, 1)
         gram[round_index, me] = pack(full)
         for device, _ in peers:
             mine = gram.at[round_index, me]
@@ -248,8 +256,7 @@
             rows = pl.ds(pl.multiple_of(c * (CHUNK_C * n_j), CHUNK_C * n_j), CHUNK_C * n_j)
             rows_a = blk_a[pl.ds(pl.multiple_of(c * CHUNK_C, CHUNK_C), CHUNK_C), :]
             paired = (rows_a[:, None, :] * block_b[None]).reshape(CHUNK_C * n_j, wide)
-            high, low = split(paired)
-            mixed = jnp.where(left_half(paired.shape), high, low).astype(jnp.bfloat16)
+            mixed = mix(paired)
             sum_c[...] += lax.dot_general(
                 mixed,
                 pair_ref[rows, :],
@@ -266,8 +273,7 @@
 
         receive(round_index, 2)
         send_gram(round_index, 2)
-        high_c, low_c = split(blk_c[...])
-        mixed_c = jnp.where(left_half((n_k, wide)), high_c, low_c).astype(jnp.bfloat16)
+        mixed_c = mix(blk_c[...])
         weights = jnp.concatenate([mixed_c, mixed_c], axis=0)
         sum_b[...] = jnp.zeros_like(sum_b)
 
@@ -290,15 +296,16 @@
         for (peers, me, which), gram in zip(lines, grams):
             all_of(gram.at[round_index], peers, 9 * round_index + 3 + which).wait_recv()
             totals.append(sum(gram[round_index, p] for p in range(len(peers) + 1)))
-        products = [
-            jnp.concatenate(unpack(totals[p] * totals[q], rank), axis=0)
-            for p, q in ((1, 2), (0, 2), (0, 1))
-        ]
-        heads = [
-            jnp.dot(x[:, :rank], product, precision=HIGHEST, preferred_element_type=jnp.float32)
-            for x, product in zip(own, products)
-        ]
         slopes = [None] * 3
+        heads = []
+        for which, (p, q) in enumerate(((1, 2), (0, 2), (0, 1))):
+            product = mix(jnp.concatenate(unpack(totals[p] * totals[q], rank), axis=0))
+            head = jnp.dot(
+                mix(own[which]),
+                jnp.concatenate([product, product], axis=0),
+                preferred_element_type=jnp.float32,
+            )
+            heads.append(head + pltpu.roll(head, rank, 1))
         for which in (2, 0, 1):
             peers = groups[which][0]
             pull, rows = pulls[which], owned[which].shape[0]
@@ -306,9 +313,9 @@
             moment = sum(pull[round_index, p] for p in range(len(peers) + 1))
             moment = jnp.concatenate(unpack(moment, rows), axis=0)
             slopes[which] = (heads[which] - moment) / counts[which]
-        if round_index + 1 < STEPS:
-            own = [x - step_size * slope for x, slope in zip(own, slopes)]
-            gather(gathers, round_index + 1, own)
+            if round_index + 1 < STEPS:
+                own[which] = own[which] - step_size * slopes[which]
+                gather(round_index + 1, which, own[which])
 
     for ref, slope in zip((out_a_ref, out_b_ref, out_c_ref), slopes):
         ref[...] = slope[:, :rank]
@@ -339,6 +346,10 @@
     sides = [ny * nz, nx * nz, nx * ny]
     slots = [pltpu.VMEM((STEPS, n, packed_rows(r), wide), f32) for n, r in zip(sides, rows)]
     blocks = [pltpu.VMEM((n, wide), f32) for n in (n_i, n_j, n_k)]
+    operands = [
+        pltpu.with_memory_space_constraint(x, pltpu.HBM)
+        for x in (tensor, factor_a, factor_b, factor_c)
+    ]
     slopes = pl.pallas_call(
         functools.partial(kernel, sizes, counts),
         out_shape=[jax.ShapeDtypeStruct(x.shape, f32) for x in (factor_a, factor_b, factor_c)],
@@ -362,16 +373,16 @@
             pltpu.SemaphoreType.DMA((9 * STEPS,)),
         ],
         compiler_params=pltpu.CompilerParams(
-            collective_id=0, has_side_effects=True, vmem_limit_bytes=60 * 1024 * 1024
+            collective_id=0, has_side_effects=True, vmem_limit_bytes=48 * 1024 * 1024
         ),
-    )(tensor, factor_a, factor_b, factor_c)
+    )(*operands)
     return pl.pallas_call(
         store,
         out_shape=[jax.ShapeDtypeStruct(x.shape, f32) for x in (factor_a, factor_b, factor_c)],
         in_specs=[pl.BlockSpec(memory_space=pl.ANY)] * 3,
         out_specs=[pl.BlockSpec(memory_space=pltpu.HBM)] * 3,
         scratch_shapes=[pltpu.SemaphoreType.DMA((3,))],
-        compiler_params=pltpu.CompilerParams(vmem_limit_bytes=60 * 1024 * 1024),
+        compiler_params=pltpu.CompilerParams(vmem_limit_bytes=48 * 1024 * 1024),
     )(*slopes)
 
 

time: 33.4 us -> 31.9 us (0.955)
  Pallas kernels: 32.6 us -> 31.1 us
    pallas_call x1, Pallas kernels: 1.63 us -> 0.63 us  [shards(): pl.pallas_call(store, out_shape=[jax.ShapeDtypeStruct(x.shape, f32) for x...]
    pallas_call x1, Pallas kernels: 31 us -> 30.5 us  [shards(): pl.pallas_call(functools.partial(kernel, sizes, counts), out_shape=[jax.S...]
where the time goes in v3:
time: 31.9 us; the launch traced here: 31.8 us
  Pallas kernels  31.1 us (97%)
  between operations  0.64 us (2%)
    pallas_call x1, Pallas kernels, shards(): pl.pallas_call(functools.partial(kernel, sizes, counts), out_shape=[jax.S...  30.5 us

profile of v3, /device:TPU:0, one launch (start us, length us, event | category | flops | bytes accessed | tf_op | source)
XLA Modules:
  0.0 31.8 jit_solution(788105782164218150)
XLA Ops:
  0.6 30.5 %shard_map.67 = (f32[16,64]{1,0:T(8,128)S(1)}, f32[8,64]{1,0:T(8,128)S(1)}, f32[8,64]{1,0:T(8,128)S(1)}) custom-call(f32[128,64,128]{2,1,0:T(8,128)} %tensor_hbm.1, f32[16,64]{1,0:T(8,128)} %own_a_hbm.1, f32[8,64]{1,0:T(8,128)} %own_b_hbm.1, f32[8,64]{1,0:T(8,128)} %own_c_hbm.1), custom_call_target="tpu_custom_call" | custom-call | tf_op jit(solution)/shard_map/pallas_call | solution.py:353
  31.1 0.6 %shard_map.68 = (f32[16,64]{1,0:T(8,128)}, f32[8,64]{1,0:T(8,128)}, f32[8,64]{1,0:T(8,128)}) custom-call(f32[16,64]{1,0:T(8,128)S(1)} %get-tuple-element.6.from_a, f32[8,64]{1,0:T(8,128)S(1)} %get-tuple-element.7.from_b, f32[8,64]{1,0:T(8,128)S(1)} %get-tuple-element.8.from_c), custom_call_target="tpu_custom_call" | custom-call | tf_op jit(solution)/shard_map/pallas_call | solution.py:379

commit v4 on v3

--- a/solution.py
+++ b/solution.py
@@ -12,6 +12,7 @@
 MESH = pl.DeviceIdType.MESH
 CHUNK = 8
 CHUNK_C = 16
+PARTS = 4
 
 
 def twice(x):
@@ -185,7 +186,7 @@
         load.wait()
     own = [twice(ref[...]) for ref in owned]
     pl.semaphore_wait(barrier, len(greeted))
-    for which in range(3):
+    for which in (1, 0, 2):
         gather(0, which, own[which])
 
     for p, load in enumerate(loads):
@@ -243,6 +244,23 @@
         pull[round_index, me] = push[round_index, me]
         finals.append((pull.at[round_index], peers, slot))
 
+    def scatter_a(round_index, part):
+        me, rows = groups[0][1], own_a_ref.shape[0]
+        places = ny * nz // PARTS
+        for p in range(part * places, (part + 1) * places):
+            moment = sum_a[p * rows : (p + 1) * rows]
+            push_a[round_index, p] = pack(moment + pltpu.roll(moment, rank, 1))
+
+            @pl.when(me != p)
+            def _():
+                device = {"gx": gx, "gy": jnp.int32(p // nz), "gz": jnp.int32(p % nz)}
+                transfer(
+                    push_a.at[round_index, p],
+                    pull_a.at[round_index, me],
+                    9 * round_index + 6,
+                    device,
+                ).start()
+
     for round_index in range(STEPS):
         receive(round_index, 0)
         receive(round_index, 1)
@@ -287,10 +305,15 @@
             sum_b[...] += jnp.sum(along * rows_a[:, None, :], axis=0)
             return carry
 
-        lax.fori_loop(0, n_i // CHUNK, contract_ab, 0, unroll=4)
-        moment_a, moment_b = sum_a[...], sum_b[...]
-        scatter(round_index, 0, moment_a + pltpu.roll(moment_a, rank, 1))
-        scatter(round_index, 1, moment_b + pltpu.roll(moment_b, rank, 1))
+        steps = n_i // CHUNK // PARTS
+        for part in range(PARTS):
+            lax.fori_loop(part * steps, (part + 1) * steps, contract_ab, 0, unroll=4)
+            if part == PARTS - 1:
+                moment_b = sum_b[...]
+                scatter(round_index, 1, moment_b + pltpu.roll(moment_b, rank, 1))
+            scatter_a(round_index, part)
+        pull_a[round_index, groups[0][1]] = push_a[round_index, groups[0][1]]
+        finals.append((pull_a.at[round_index], peers_a, 9 * round_index + 6))
 
         totals = []
         for (peers, me, which), gram in zip(lines, grams):

time: 31.9 us -> 32.1 us (level)
  no operation moved by 1% of the time
where the time goes in v4:
time: 32.1 us; the launch traced here: 31.9 us
  Pallas kernels  31.3 us (98%)
  between operations  0.64 us (2%)
    pallas_call x1, Pallas kernels, shards(): pl.pallas_call(functools.partial(kernel, sizes, counts), out_shape=[jax.S...  30.7 us

profile of v4, /device:TPU:0, one launch (start us, length us, event | category | flops | bytes accessed | tf_op | source)
XLA Modules:
  0.0 31.9 jit_solution(5236305643748144616)
XLA Ops:
  0.6 30.7 %shard_map.67 = (f32[16,64]{1,0:T(8,128)S(1)}, f32[8,64]{1,0:T(8,128)S(1)}, f32[8,64]{1,0:T(8,128)S(1)}) custom-call(f32[128,64,128]{2,1,0:T(8,128)} %tensor_hbm.1, f32[16,64]{1,0:T(8,128)} %own_a_hbm.1, f32[8,64]{1,0:T(8,128)} %own_b_hbm.1, f32[8,64]{1,0:T(8,128)} %own_c_hbm.1), custom_call_target="tpu_custom_call" | custom-call | tf_op jit(solution)/shard_map/pallas_call | solution.py:376
  31.3 0.6 %shard_map.68 = (f32[16,64]{1,0:T(8,128)}, f32[8,64]{1,0:T(8,128)}, f32[8,64]{1,0:T(8,128)}) custom-call(f32[16,64]{1,0:T(8,128)S(1)} %get-tuple-element.6.from_a, f32[8,64]{1,0:T(8,128)S(1)} %get-tuple-element.7.from_b, f32[8,64]{1,0:T(8,128)S(1)} %get-tuple-element.8.from_c), custom_call_target="tpu_custom_call" | custom-call | tf_op jit(solution)/shard_map/pallas_call | solution.py:402

commit v5 on v3

--- a/solution.py
+++ b/solution.py
@@ -265,7 +265,7 @@
             )
             return carry
 
-        lax.fori_loop(0, n_i // CHUNK_C, contract_c, 0, unroll=2)
+        lax.fori_loop(0, n_i // CHUNK_C, contract_c, 0, unroll=4)
         flipped = sum_c[...]
         flipped = flipped[:, :n_k] + flipped[:, n_k:]
         flipped = flipped[:rank] + flipped[rank:]
@@ -287,7 +287,7 @@
             sum_b[...] += jnp.sum(along * rows_a[:, None, :], axis=0)
             return carry
 
-        lax.fori_loop(0, n_i // CHUNK, contract_ab, 0, unroll=4)
+        lax.fori_loop(0, n_i // CHUNK, contract_ab, 0, unroll=8)
         moment_a, moment_b = sum_a[...], sum_b[...]
         scatter(round_index, 0, moment_a + pltpu.roll(moment_a, rank, 1))
         scatter(round_index, 1, moment_b + pltpu.roll(moment_b, rank, 1))

time: 31.9 us -> 30.5 us (0.956)
  Pallas kernels: 31.1 us -> 29.7 us
    pallas_call x1, Pallas kernels: 30.5 us -> 29 us  [shards(): pl.pallas_call(functools.partial(kernel, sizes, counts), out_shape=[jax.S...]
where the time goes in v5:
time: 30.5 us; the launch traced here: 30.3 us
  Pallas kernels  29.7 us (97%)
  between operations  0.64 us (2%)
    pallas_call x1, Pallas kernels, shards(): pl.pallas_call(functools.partial(kernel, sizes, counts), out_shape=[jax.S...  29 us
    pallas_call x1, Pallas kernels, shards(): pl.pallas_call(store, out_shape=[jax.ShapeDtypeStruct(x.shape, f32) for x...  0.63 us

profile of v5, /device:TPU:0, one launch (start us, length us, event | category | flops | bytes accessed | tf_op | source)
XLA Modules:
  0.0 30.3 jit_solution(420094386252765486)
XLA Ops:
  0.6 29.0 %shard_map.67 = (f32[16,64]{1,0:T(8,128)S(1)}, f32[8,64]{1,0:T(8,128)S(1)}, f32[8,64]{1,0:T(8,128)S(1)}) custom-call(f32[128,64,128]{2,1,0:T(8,128)} %tensor_hbm.1, f32[16,64]{1,0:T(8,128)} %own_a_hbm.1, f32[8,64]{1,0:T(8,128)} %own_b_hbm.1, f32[8,64]{1,0:T(8,128)} %own_c_hbm.1), custom_call_target="tpu_custom_call" | custom-call | tf_op jit(solution)/shard_map/pallas_call | solution.py:353
  29.7 0.6 %shard_map.68 = (f32[16,64]{1,0:T(8,128)}, f32[8,64]{1,0:T(8,128)}, f32[8,64]{1,0:T(8,128)}) custom-call(f32[16,64]{1,0:T(8,128)S(1)} %get-tuple-element.6.from_a, f32[8,64]{1,0:T(8,128)S(1)} %get-tuple-element.7.from_b, f32[8,64]{1,0:T(8,128)S(1)} %get-tuple-element.8.from_c), custom_call_target="tpu_custom_call" | custom-call | tf_op jit(solution)/shard_map/pallas_call | solution.py:379
